TPU v7x, 32 devices: a whole 2x2x4 slice. The times are simulated.
32 devices in a mesh: groups: 2 (over y), ctx: 4 (over z), tp: 4 (over x, core).
Axes of the slice: x: 2, y: 2, z: 4, core: 2. Of those that a mesh axis runs over, the one named last changes fastest.
Arguments:
- queries: bfloat16 [2048, 64, 128], P(('groups', 'ctx'), 'tp'), parts along dimension 0, may hold values from -4.5 to 4.5
- keys: bfloat16 [2048, 8, 128], P(('groups', 'ctx'), 'tp'), parts along dimension 0, may hold values from -5.5 to 5.5
- values: bfloat16 [2048, 8, 128], P(('groups', 'ctx'), 'tp'), parts along dimension 0, may hold values from -6 to 6
- doc_pos: int32 [2048], P(('groups', 'ctx')), parts along dimension 0, may hold values from 0 to 511, as said below
- log_decay: float32 [2048, 64], P(('groups', 'ctx'), 'tp'), parts along dimension 0, may hold values from -0.8 to 0
- student_c: bfloat16 [2048, 64, 128], P(('groups', 'ctx'), 'tp'), parts along dimension 0, may hold values from -6 to 6
- student_write: bfloat16 [2048, 8, 128], P(('groups', 'ctx'), 'tp'), parts along dimension 0, may hold values from -6 to 6
- student_input: bfloat16 [2048, 8, 128], P(('groups', 'ctx'), 'tp'), parts along dimension 0, may hold values from -46 to 46
- gain: float32 [64, 128], P('tp'), may hold values from 0.5 to 1.5
Outputs:
- readout_gradient: bfloat16 [2048, 64, 128], P(('groups', 'ctx'), 'tp'), parts along dimension 0
- write_gradient: bfloat16 [2048, 8, 128], P(('groups', 'ctx'), 'tp'), parts along dimension 0
- input_gradient: bfloat16 [2048, 8, 128], P(('groups', 'ctx'), 'tp'), parts along dimension 0
- grad_gain: float32 [128, 128], P(('groups', 'tp')), parts along dimension 0
There are 2 independent parts, one for each index of `groups`. A program takes and returns all parts, laid end to end along the dimension named above; an argument that names none is the same for every part. Nothing has to cross between parts.
Inputs may be any that keep to these rules, and one draw needn't show every extreme that they name: `doc_pos`: every document starts with position 0 and counts up by one a token; the first token starts a document; the longest document has exactly 512 tokens.
All inputs are finite; a program needn't handle non-finite values.
Results may differ from a plain program's by a relative error of at most 0.0075.
Values may be sent and summed in bfloat16 or wider, within the bound.
A program may use at most 128 MiB of HBM per device.

v0:
```python
import math

import jax
import jax.numpy as jnp
from jax import lax
from jax.sharding import PartitionSpec as P

EPSILON = 1e-05
STUDENT_FLOOR = 1.0
NEG_FLOOR = -1e30


def entering(value, axis, join, neutral, backward):
    count, mine = (lax.axis_size(axis), lax.axis_index(axis))
    pieces = jax.tree.map(lambda part: lax.all_gather(part, axis), value)
    if backward:
        pieces = jax.tree.map(lambda part: part[::-1], pieces)
        mine = count - 1 - mine
    so_far = jax.tree.map(
        lambda part, zero: jnp.full_like(part, 0) + jnp.asarray(zero, part.dtype), value, neutral
    )

    def step(position, so_far):
        longer = join(so_far, jax.tree.map(lambda part: part[position], pieces))
        return jax.tree.map(lambda new, old: jnp.where(position < mine, new, old), longer, so_far)

    return lax.fori_loop(0, count - 1, step, so_far)


def chain_states(earlier, later):
    decay_one, state_one = earlier
    decay_two, state_two = later
    return (decay_one * decay_two, decay_two[:, None, None] * state_one + state_two)


def attend_block(running, key_tile, value_block, key_first, queries, positions, doc_start):
    best, accum = running
    tok_rows, head_count, head_width = queries.shape
    group_count = key_tile.shape[1]
    repeat = head_count // group_count
    block_rows = key_tile.shape[0]
    key_positions = key_first + jnp.arange(block_rows, dtype=jnp.int32)
    visible = (key_positions[None, :] <= positions[:, None]) & (
        key_positions[None, :] >= doc_start[:, None]
    )
    grouped_rows = queries.reshape(tok_rows, group_count, repeat, head_width)
    score_matrix = jnp.einsum(
        "yubk,ouk->ubyo", grouped_rows, key_tile, preferred_element_type=jnp.float32
    )
    score_matrix = score_matrix.reshape(head_count, tok_rows, block_rows) * (
        1.0 / math.sqrt(head_width)
    )
    score_matrix = jnp.where(visible[None], score_matrix, -jnp.inf)
    new_best = jnp.maximum(best, jnp.max(score_matrix, axis=-1))
    weights = jnp.exp(score_matrix - new_best[..., None]).astype(jnp.bfloat16)
    mixed_out = jnp.einsum(
        "hvbc,chw->hvbw",
        weights.reshape(group_count, repeat, tok_rows, block_rows),
        value_block,
        preferred_element_type=jnp.float32,
    )
    accum = accum * jnp.exp(best - new_best)[..., None] + mixed_out.reshape(
        head_count, tok_rows, head_width
    )
    return (new_best, accum)


def fold_keys(running, pieces, queries, positions, doc_start):
    key_rows, value_rows = pieces
    count = key_rows.shape[0]
    block_rows = math.gcd(count, 512)
    lowest = jnp.min(doc_start)
    highest = positions[-1]

    def one_step(current, block_index):
        key_first = block_index * block_rows
        key_tile = lax.dynamic_slice_in_dim(key_rows, block_index * block_rows, block_rows, 0)
        value_block = lax.dynamic_slice_in_dim(value_rows, block_index * block_rows, block_rows, 0)
        needed = (key_first <= highest) & (key_first + block_rows - 1 >= lowest)

        def update(inside):
            return attend_block(
                inside, key_tile, value_block, key_first, queries, positions, doc_start
            )

        def unchanged(inside):
            return inside

        return (lax.cond(needed, update, unchanged, current), None)

    result, _ = lax.scan(one_step, running, jnp.arange(count // block_rows, dtype=jnp.int32))
    return result


def body(queries, keys, values, doc_pos, log_decay, student_c, student_write, student_input, gain):
    tok_rows, head_count, head_width = queries.shape
    group_count = keys.shape[1]
    repeat = head_count // group_count
    state_width = student_c.shape[2]
    ctx_count = lax.axis_size("ctx")
    first_row = lax.axis_index("ctx") * tok_rows
    positions = first_row + jnp.arange(tok_rows, dtype=jnp.int32)
    doc_start = positions - doc_pos
    start_state = (
        jnp.full((head_count, tok_rows), NEG_FLOOR, jnp.float32),
        jnp.zeros((head_count, tok_rows, head_width), jnp.float32),
    )
    best, accum = fold_keys(
        start_state,
        (
            lax.all_gather(keys, "ctx", axis=0, tiled=True),
            lax.all_gather(values, "ctx", axis=0, tiled=True),
        ),
        queries,
        positions,
        doc_start,
    )
    teacher = accum / jnp.sqrt(jnp.mean(accum * accum, axis=-1, keepdims=True) + EPSILON)
    target = teacher.astype(jnp.bfloat16).transpose(1, 0, 2)
    log_level = jnp.cumsum(log_decay, axis=0)
    level_rows = log_level.T
    same_doc = (positions[None, :] <= positions[:, None]) & (
        positions[None, :] >= doc_start[:, None]
    )
    fade = jnp.exp(
        jnp.where(same_doc[None], level_rows[:, :, None] - level_rows[:, None, :], -jnp.inf)
    )
    grouped_readout = student_c.reshape(tok_rows, group_count, repeat, state_width)
    inner_product = jnp.einsum(
        "oizy,eiy->izoe", grouped_readout, student_write, preferred_element_type=jnp.float32
    )
    decay_kernel = (fade * inner_product.reshape(head_count, tok_rows, tok_rows)).astype(
        jnp.bfloat16
    )
    grouped_matrix = decay_kernel.reshape(group_count, repeat, tok_rows, tok_rows)
    within_block = jnp.einsum(
        "dlmx,xdc->mdlc", grouped_matrix, student_input, preferred_element_type=jnp.float32
    )
    within_block = within_block.reshape(tok_rows, head_count, head_width)
    last_start = doc_start[-1]
    tail_fade = jnp.where(
        (positions >= last_start)[:, None], jnp.exp(log_level[-1:, :] - log_level), 0.0
    )
    scaled_b = (
        tail_fade.reshape(tok_rows, group_count, repeat)[..., None] * student_write[:, :, None, :]
    ).astype(jnp.bfloat16)
    block_state = jnp.einsum(
        "tgrn,tgp->grnp", scaled_b, student_input, preferred_element_type=jnp.float32
    )
    block_state = block_state.reshape(head_count, state_width, head_width)
    block_decay = jnp.where(last_start < first_row, jnp.exp(log_level[-1]), 0.0)
    identity = (
        jnp.ones((head_count,), jnp.float32),
        jnp.zeros((head_count, state_width, head_width), jnp.float32),
    )
    _, carry_in = entering((block_decay, block_state), "ctx", chain_states, identity, False)
    head_fade = jnp.where((doc_start < first_row)[:, None], jnp.exp(log_level), 0.0)
    carry_low = carry_in.astype(jnp.bfloat16)
    from_carry = (
        jnp.einsum("thn,hnp->thp", student_c, carry_low, preferred_element_type=jnp.float32)
        * head_fade[..., None]
    )
    mixer = within_block + from_carry
    root_mean = jnp.sqrt(jnp.mean(mixer * mixer, axis=-1, keepdims=True) + STUDENT_FLOOR)
    normed = mixer / root_mean
    residual_diff = normed * gain[None] - target.astype(jnp.float32)
    gain_term = jnp.sum(residual_diff * normed, axis=0) / (tok_rows * ctx_count)
    grad_gain = lax.psum(gain_term, "ctx")
    scaled_diff = residual_diff * gain[None]
    mixer_grad = (
        (scaled_diff - normed * jnp.mean(scaled_diff * normed, axis=-1, keepdims=True)) / root_mean
    ).astype(jnp.bfloat16)
    faded_c = (head_fade[..., None] * student_c).astype(jnp.bfloat16)
    back_state = jnp.einsum("thn,thp->hnp", faded_c, mixer_grad, preferred_element_type=jnp.float32)
    _, carry_back = entering((block_decay, back_state), "ctx", chain_states, identity, True)
    back_low = carry_back.astype(jnp.bfloat16)
    grouped_gradient = mixer_grad.reshape(tok_rows, group_count, repeat, head_width)
    gradient_product = jnp.einsum(
        "zmhx,jmx->mhzj", grouped_gradient, student_input, preferred_element_type=jnp.float32
    )
    kernel_gradient = (fade * gradient_product.reshape(head_count, tok_rows, tok_rows)).astype(
        jnp.bfloat16
    )
    kernel_gradient = kernel_gradient.reshape(group_count, repeat, tok_rows, tok_rows)
    readout_gradient = jnp.einsum(
        "cmdu,ucx->dcmx", kernel_gradient, student_write, preferred_element_type=jnp.float32
    )
    readout_gradient = readout_gradient.reshape(tok_rows, head_count, state_width)
    readout_gradient = readout_gradient + head_fade[..., None] * jnp.einsum(
        "thp,hnp->thn", mixer_grad, carry_low, preferred_element_type=jnp.float32
    )
    grouped_fade = tail_fade.reshape(tok_rows, group_count, repeat, 1)
    grouped_back = back_low.reshape(group_count, repeat, state_width, head_width)
    write_gradient = jnp.einsum(
        "uyzx,zuye->xue", kernel_gradient, grouped_readout, preferred_element_type=jnp.float32
    )
    write_gradient = write_gradient + jnp.sum(
        grouped_fade
        * jnp.einsum(
            "grnp,sgp->sgrn", grouped_back, student_input, preferred_element_type=jnp.float32
        ),
        axis=2,
    )
    input_gradient = jnp.einsum(
        "uomb,muoz->buz", grouped_matrix, grouped_gradient, preferred_element_type=jnp.float32
    )
    input_gradient = input_gradient + jnp.sum(
        grouped_fade
        * jnp.einsum(
            "sgn,grnp->sgrp", student_write, grouped_back, preferred_element_type=jnp.float32
        ),
        axis=2,
    )
    return (
        readout_gradient.astype(jnp.bfloat16),
        write_gradient.astype(jnp.bfloat16),
        input_gradient.astype(jnp.bfloat16),
        grad_gain,
    )


def solution(mesh):
    placed = (
        P(("groups", "ctx"), "tp", None),
        P(("groups", "ctx"), "tp", None),
        P(("groups", "ctx"), "tp", None),
        P(("groups", "ctx")),
        P(("groups", "ctx"), "tp"),
        P(("groups", "ctx"), "tp", None),
        P(("groups", "ctx"), "tp", None),
        P(("groups", "ctx"), "tp", None),
        P("tp", None),
    )
    return jax.shard_map(
        body,
        mesh=mesh,
        in_specs=placed,
        out_specs=(
            P(("groups", "ctx"), "tp", None),
            P(("groups", "ctx"), "tp", None),
            P(("groups", "ctx"), "tp", None),
            P(("groups", "tp"), None),
        ),
        check_vma=False,
    )
```

profile of v0, /device:TPU:0, one launch (start us, length us, event | category | flops | bytes accessed | tf_op | source)
XLA Modules:
  0.0 225.4 jit_solution(7501806901297974506)
XLA Ops:
  12.1 2.4 %fusion.27 = f32[2,8,128,128]{3,2,1,0:T(8,128)} fusion(f32[256,2,128]{0,2,1:T(8,128)S(1)} %copy.120, f32[256,2,8]{0,2,1:T(8,128)S(1)} %get-tuple-element.705, bf16[256,2,128,1]{2,1,0,3:T(2,128)(2,1)} %bitcast.176), kind=kOutput, calls=%fused_computation.58 | convolution fusion | flops 135266304 | bytes 1458176 | tf_op jit(solution)/shard_map/tgrn,tgp->grnp/dot_general | solution.py:147
  14.8 1.6 copy.136
  18.9 24.2 %all_gather.23 = bf16[1024,2,128]{2,0,1:T(8,128)(2,1)} all-gather(bf16[256,2,128]{2,0,1:T(8,128)(2,1)S(1)} %copy.124), channel_id=1, replica_groups=mesh['groups'=2,'ctx'=4,'tp'=4] {'ctx'}, dimensions={0}, use_global_device_ids=true | all-gather | bytes 655360 | tf_op jit(solution)/shard_map/all_gather | solution.py:111
  43.2 21.8 %all_gather.24 = bf16[1024,2,128]{2,0,1:T(8,128)(2,1)} all-gather(bf16[256,2,128]{2,0,1:T(8,128)(2,1)S(1)} %copy.125), channel_id=1, replica_groups=mesh['groups'=2,'ctx'=4,'tp'=4] {'ctx'}, dimensions={0}, use_global_device_ids=true | all-gather | bytes 655360 | tf_op jit(solution)/shard_map/all_gather | solution.py:112
  65.2 11.3 %while.45 = (s32[]{:T(128)}, f32[16,256]{1,0:T(8,128)S(1)}, f32[16,256,128]{2,1,0:T(8,128)S(1)}, s32[2]{0:T(128)S(1)}, s32[]{:T(128)}, /*index=5*/s32[]{:T(128)}...) while((s32[]{:T(128)}, f32[16,256]{1,0:T(8,128)S(1)}, ...), condition=%wide.region_10.11_spmd.clone, body=%wide.region_6.10_spmd.clone.sunk | while | flops 1089868544 | bytes 29353344 | solution.py:91
  67.6 6.5 %conditional.3 = ((f32[16,256]{1,0:T(8,128)S(1)}, f32[16,256,128]{2,1,0:T(8,128)S(1)})) conditional(s32[]{:T(128)} %convert_element_type.113, (f32[16,256]{1,0:T(8,128)S(1)}, f32[16,256,128]{2,1,0:T(8,128)S(1)}) %tuple.134, (s32[]{:T(128)}, s32[]{:T(128)}, s32[256]{0:T(256)S(1)}, bf16[1024,2,128]{2,0,1:T(8,128)(2,1)}, ...), branch_computations={%region_7.7_spmd, %region_8.9_spmd} | conditional | flops 1089868544 | bytes 29352038 | solution.py:89
  67.8 2.7 %fusion.2 = (f32[2,8,256]{2,1,0:T(8,128)S(1)}, f32[2,512,256,8]{2,1,3,0:T(8,128)S(1)}) fusion(pred[256,512]{0,1:T(8,128)(4,1)S(1)} %compare_and_fusion, bf16[256,2,8,128]{3,0,2,1:T(8,128)(2,1)} %bitcast.163, bf16[1024,2,128]{2,0,1:T(8,128)(2,1)} %get-tuple-element.492, s32[]{:T(128)S(6)} %select_n.74), kind=kOutput, calls=%fused_computation.3 | convolution fusion | flops 543158272 | bytes 9846788 | tf_op jit(solution)/shard_map/while/body/eval_jaxpr/cond/branch_1_fun/yubk,ouk->ubyo/dot_general | solution.py:47
  70.5 2.5 %fusion.3 = f32[2,8,256,128]{3,2,1,0:T(8,128)S(1)} fusion(f32[2,512,256,8]{2,1,3,0:T(8,128)S(1)} %get-tuple-element.704, f32[2,8,256]{2,1,0:T(8,128)S(1)} %bitcast.170, pred[256,512]{0,1:T(8,128)(4,1)S(1)} %compare_and_fusion, bf16[1024,2,128]{2,0,1:T(8,128)(2,1)S(1)} %copy-done.12, s32[]{:T(128)S(6)} %select_n.74), kind=kOutput, calls=%fused_computation.4 | convolution fusion | flops 545259520 | bytes 10895364 | tf_op jit(solution)/shard_map/while/body/eval_jaxpr/cond/branch_1_fun/hvbc,chw->hvbw/dot_general | solution.py:56
  76.5 1.9 copy.127
  78.3 14.2 %all-gather.1 = f32[4,1,16]{2,1,0:T(1,128)S(1)} all-gather(f32[1,1,16]{2,1,0:T(1,128)S(1)} %bitcast.181), channel_id=1, replica_groups=mesh['groups'=2,'ctx'=4,'tp'=4] {'ctx'}, dimensions={0}, use_global_device_ids=true | all-gather | bytes 320 | tf_op jit(solution)/shard_map/all_gather | solution.py:15
  96.1 1.8 fusion.39
  97.9 13.4 %all-gather.5.cloned.1.call-done = f32[4,16,128,128]{3,2,1,0:T(8,128)} async-done(((f32[1,16,128,128]{3,2,1,0:T(8,128)}), f32[4,16,128,128]{3,2,1,0:T(8,128)}) %all-gather.5.cloned.1.call-update) | async-done | bytes 4194320 | tf_op jit(solution)/shard_map/all_gather | solution.py:15
  111.3 4.5 %while.46 = (s32[]{:T(128)}, f32[16,128,128]{2,1,0:T(8,128)S(1)}, s32[]{:T(128)}, f32[4,16]{1,0:T(4,128)S(1)}, f32[4,16,128,128]{3,2,1,0:T(8,128)}, /*index=5*/s32[]{:T(128)}, s32[]{:T(128)}) while((s32[]{:T(128)}, f32[16,128,128]{2,1,0:T(8,128)S(1)}, s32[]{:T(128)}, f32[4,16]{1,0:T(4,128)S(1)}, f32[4,16,128,128]{3,2,1,0:T(8,128)}, ...), condition=%wide.region_3.4_spmd.clone, body=%wide.region_2.0_spmd.clone.sunk | while | flops 1048580 | bytes 3146025 | solution.py:27
  111.3 1.5 fusion.65
  115.8 2.3 %multiply_reduce_fusion.3 = (f32[256,16]{0,1:T(8,128)S(1)}, f32[256,16,128]{0,2,1:T(8,128)S(1)}) fusion(f32[256,16]{0,1:T(8,128)S(1)} %get-tuple-element.706, bf16[256,16,128]{0,2,1:T(8,128)(2,1)S(1)} %copy-done.1, f32[16,128,128]{2,1,0:T(8,128)S(1)} %get-tuple-element.523, f32[2,8,256,128]{2,3,1,0:T(8,128)} %fusion.39), kind=kOutput, calls=%fused_computation.49 | convolution fusion | flops 136572928 | bytes 6324224 | tf_op jit(solution)/shard_map/thn,hnp->thp/dot_general | solution.py:160
  124.3 2.3 %convolution_bitcast_fusion = f32[256,2,8,128]{3,0,2,1:T(8,128)} fusion(bf16[2,8,256,256]{2,3,1,0:T(8,128)(2,1)S(1)} %fusion.16, bf16[256,2,128,1]{2,1,0,3:T(2,128)(2,1)S(1)} %bitcast.174), kind=kOutput, calls=%fused_computation.51 | convolution fusion | flops 268435456 | bytes 4325376 | tf_op jit(solution)/shard_map/cmdu,ucx->dcmx/dot_general | solution.py:185
  126.6 3.0 %copy.133 = f32[256,2,8,128]{0,3,2,1:T(8,128)} copy(f32[256,2,8,128]{3,0,2,1:T(8,128)} %convolution_bitcast_fusion) | data formatting | bytes 4194304 | tf_op jit(solution)/shard_map/cmdu,ucx->dcmx/transpose | solution.py:185
  129.5 3.1 %fusion.21 = bf16[256,16,128]{0,2,1:T(8,128)(2,1)} fusion(f32[256,2,8,128]{0,3,2,1:T(8,128)} %copy.133, bf16[256,16,128]{0,2,1:T(8,128)(2,1)S(1)} %divide_convert_fusion, f32[256,16]{0,1:T(8,128)S(1)} %get-tuple-element.706, f32[16,128,128]{2,1,0:T(8,128)S(1)} %get-tuple-element.523), kind=kOutput, calls=%fused_computation.39 | convolution fusion | flops 136052736 | bytes 5259264 | tf_op jit(solution)/shard_map/thp,hnp->thn/dot_general | solution.py:189
  132.7 2.6 %copy.143 = bf16[256,16,128]{2,1,0:T(8,128)(2,1)} copy(bf16[256,16,128]{0,2,1:T(8,128)(2,1)} %fusion.21) | data formatting | bytes 2097152
  135.3 11.9 %psum.7 = f32[16,128]{1,0:T(8,128)} all-reduce(f32[16,128]{1,0:T(8,128)S(1)} %broadcast_multiply_fusion.1), channel_id=1, replica_groups=mesh['groups'=2,'ctx'=4,'tp'=4] {'ctx'}, use_global_device_ids=true, to_apply=%region_18.19 | all-reduce | flops 2048 | bytes 16384 | tf_op jit(solution)/shard_map/psum | solution.py:168
  147.2 55.8 %all-gather.7.cloned.1.call-done = f32[64,128,128]{2,1,0:T(8,128)} async-done(((f32[16,128,128]{2,1,0:T(8,128)}), f32[64,128,128]{2,1,0:T(8,128)}) %all-gather.7.cloned.1.call-update) | async-done | bytes 4194320 | tf_op jit(solution)/shard_map/all_gather | solution.py:15
  203.0 4.7 %rev.7 = f32[4,16,128,128]{3,2,1,0:T(8,128)} reverse(f32[4,16,128,128]{3,2,1,0:T(8,128)} %bitcast.168), dimensions={0} | reverse | bytes 8388608 | tf_op jit(solution)/shard_map/rev | solution.py:17
  207.6 4.5 %while.47 = (s32[]{:T(128)}, f32[16,128,128]{2,1,0:T(8,128)S(1)}, s32[]{:T(128)}, f32[4,16]{1,0:T(4,128)S(1)}, f32[4,16,128,128]{3,2,1,0:T(8,128)}, /*index=5*/s32[]{:T(128)}, s32[]{:T(128)}) while((s32[]{:T(128)}, f32[16,128,128]{2,1,0:T(8,128)S(1)}, s32[]{:T(128)}, f32[4,16]{1,0:T(4,128)S(1)}, f32[4,16,128,128]{3,2,1,0:T(8,128)}, ...), condition=%wide.region_14.15_spmd.clone, body=%wide.region_13.14_spmd.clone.sunk | while | flops 1048580 | bytes 3146025 | solution.py:27
  215.4 2.3 %fusion.26 = bf16[256,2,128]{2,0,1:T(8,128)(2,1)S(1)} fusion(f32[256,2,128]{2,0,1:T(8,128)S(1)} %copy.139, bf16[2,8,256,256]{2,3,1,0:T(8,128)(2,1)} %copy-done.4, bf16[256,2,8,128]{3,2,1,0:T(8,128)(2,1)S(1)} %bitcast.167), kind=kOutput, calls=%fused_computation.57 | convolution fusion | flops 268566528 | bytes 3538944 | tf_op jit(solution)/shard_map/uyzx,zuye->xue/dot_general | solution.py:194
  (102 shorter events, 30.5 us)
Async XLA Ops:
  7.2 2.7 %copy-start = (f32[256,16]{0,1:T(8,128)S(1)}, f32[256,16]{0,1:T(8,128)}, u32[]{:S(2)}) copy-start(f32[256,16]{0,1:T(8,128)} %param.21) | copy-start | bytes 49156
  7.2 7.6 %copy-start.6 = (bf16[256,16,128]{2,1,0:T(8,128)(2,1)S(1)}, bf16[256,16,128]{2,1,0:T(8,128)(2,1)}, u32[]{:S(2)}) copy-start(bf16[256,16,128]{2,1,0:T(8,128)(2,1)} %param.22) | copy-start | bytes 3145732
  7.2 104.1 %all-gather.5.cloned.1.call-start = ((), (), s32[]{:S(2)}) async-start(), calls=%async_computation | async-start | bytes 5242880 | tf_op jit(solution)/shard_map/all_gather | solution.py:15
  12.1 5.5 %copy-start.9 = (bf16[256,16,128]{2,1,0:T(8,128)(2,1)S(1)}, bf16[256,16,128]{2,1,0:T(8,128)(2,1)}, u32[]{:S(2)}) copy-start(bf16[256,16,128]{2,1,0:T(8,128)(2,1)} %param.17) | copy-start | bytes 3145732
  14.6 188.4 %all-gather.7.cloned.1.call-start = ((), (), s32[]{:S(2)}) async-start(), calls=%async_computation.1 | async-start | bytes 5242880 | tf_op jit(solution)/shard_map/all_gather | solution.py:15
  14.8 4.1 %copy-start.13 = (bf16[256,2,128]{2,1,0:T(2,128)(2,1)S(1)}, bf16[256,2,128]{2,1,0:T(2,128)(2,1)}, u32[]{:S(2)}) copy-start(bf16[256,2,128]{2,1,0:T(2,128)(2,1)} %param.18) | copy-start | bytes 393220
  14.8 4.1 %copy-start.14 = (bf16[256,2,128]{2,1,0:T(2,128)(2,1)S(1)}, bf16[256,2,128]{2,1,0:T(2,128)(2,1)}, u32[]{:S(2)}) copy-start(bf16[256,2,128]{2,1,0:T(2,128)(2,1)} %param.19) | copy-start | bytes 393220
  67.8 2.8 %copy-start.12 = (bf16[1024,2,128]{2,0,1:T(8,128)(2,1)S(1)}, bf16[1024,2,128]{2,0,1:T(8,128)(2,1)}, u32[]{:S(2)}) copy-start(bf16[1024,2,128]{2,0,1:T(8,128)(2,1)} %get-tuple-element.495) | copy-start | bytes 1572868 | tf_op jit(solution)/shard_map/while/body/eval_jaxpr/cond
  78.3 14.9 %copy-start.7 = (bf16[256,16,128]{2,1,0:T(8,128)(2,1)S(1)}, bf16[256,16,128]{2,1,0:T(8,128)(2,1)}, u32[]{:S(2)}) copy-start(bf16[256,16,128]{2,1,0:T(8,128)(2,1)} %param.22) | copy-start | bytes 3145732
  78.3 14.9 %copy-start.10 = (bf16[256,2,128]{2,1,0:T(2,128)(2,1)S(1)}, bf16[256,2,128]{2,1,0:T(2,128)(2,1)}, u32[]{:S(2)}) copy-start(bf16[256,2,128]{2,1,0:T(2,128)(2,1)} %param.23) | copy-start | bytes 393220
  93.3 2.8 %copy-start.11 = (bf16[256,2,128]{2,1,0:T(2,128)(2,1)S(1)}, bf16[256,2,128]{2,1,0:T(2,128)(2,1)}, u32[]{:S(2)}) copy-start(bf16[256,2,128]{2,1,0:T(2,128)(2,1)} %param.24) | copy-start | bytes 393220
  94.7 1.4 copy-start.2
  111.3 4.6 %copy-start.1 = (bf16[256,16,128]{0,2,1:T(8,128)(2,1)S(1)}, bf16[256,16,128]{0,2,1:T(8,128)(2,1)}, u32[]{:S(2)}) copy-start(bf16[256,16,128]{0,2,1:T(8,128)(2,1)} %copy.136) | copy-start | bytes 3145732
  115.8 2.4 %copy-start.5 = (f32[16,256,128]{1,2,0:T(8,128)S(1)}, f32[16,256,128]{1,2,0:T(8,128)}, u32[]{:S(2)}) copy-start(f32[16,256,128]{1,2,0:T(8,128)} %copy.127) | copy-start | bytes 6291460
  115.8 2.4 %copy-start.15 = (f32[16,128]{1,0:T(8,128)S(1)}, f32[16,128]{1,0:T(8,128)}, u32[]{:S(2)}) copy-start(f32[16,128]{1,0:T(8,128)} %param.25) | copy-start | bytes 24580
  123.0 1.3 copy-start.4
  212.1 1.6 copy-start.3
  213.7 1.7 copy-start.8
Sparse Core Ops, SparseCore 0:
  14.7 96.5 all-gather.4
  121.8 81.0 all-gather.6
where the time goes:
time: 226 us; the launch traced here: 225 us
  blocking collectives  72 us (32%)
  waiting for transfers between devices  69.2 us (31%)
  matrix products  25.4 us (11%)
  local copies, waits for them, and re-layouts  23.8 us (11%)
  other arithmetic  15.9 us (7%)
  between operations  15.1 us (7%)
  loops' own time  3.88 us (2%)
    all_gather x2, waiting for transfers between devices, entering(): pieces = jax.tree.map(lambda part: lax.all_gather(part, axis), value)  69.1 us
    all_gather x1, blocking collectives, body(): lax.all_gather(keys, 'ctx', axis=0, tiled=True)  24.2 us
    all_gather x1, blocking collectives, body(): lax.all_gather(values, 'ctx', axis=0, tiled=True)  21.8 us
    all_gather x1, blocking collectives, entering(): pieces = jax.tree.map(lambda part: lax.all_gather(part, axis), value)  14.2 us
    psum x1, blocking collectives, body(): grad_gain = lax.psum(gain_term, 'ctx')  11.9 us
    unnamed x37, local copies, waits for them, and re-layouts  10.3 us
    select_n x6, other arithmetic, step(): jnp.where(position < mine, new, old)  8.83 us
    rev x2, local copies, waits for them, and re-layouts, entering(): pieces = jax.tree.map(lambda part: part[::-1], pieces)  4.68 us
  transfers between devices with their start and end apart: 2, of which 2 were waited for; matrix products, arithmetic and copies ran while one was open for 13% of the time, Pallas kernels for 0%

commit v1 on v0

v1 whole, which is shorter than its diff:
```python
import functools
import math

import jax
import jax.numpy as jnp
from jax import lax
from jax.experimental import pallas as pl
from jax.experimental.pallas import tpu as pltpu
from jax.sharding import PartitionSpec as P

EPSILON = 1e-05
STUDENT_FLOOR = 1.0
HIDDEN = -1e30
LANES = 128
F32 = jnp.float32
BF16 = jnp.bfloat16
MESH = pl.DeviceIdType.MESH
WRITE, INPUT, KEY, VALUE = range(4)
ARRAYS = 4


def nn(a, b):
    return jnp.dot(a, b, preferred_element_type=F32)


def nt(a, b):
    return lax.dot_general(a, b, (((1,), (1,)), ((), ())), preferred_element_type=F32)


def wide(column, width):
    return column if width == LANES else jnp.concatenate([column] * (width // LANES), axis=1)


def column_of(row):
    return jnp.broadcast_to(row, (LANES, row.shape[1])).T


def kernel(
    n, reach,
    q_ref, c_ref, pack_ref, decay_ref, pos_ref, gain_ref,
    readout_ref, write_ref, input_ref, gain_out_ref,
    halo, own_tail, own_decay, own_rows, halo_rows, level, head_rows, faded_tail, halo_wt,
    c_t, fade, kern, intra, accum, best, head_col, bias,
    own_back, send_back, recv_back, write_t, input_t, gain_sum, gain_slots,
    halo_send, halo_recv, back_send, back_recv, gain_send, gain_recv,
):
    heads, tokens, width = q_ref.shape
    groups = pack_ref.shape[1]
    repeat = heads // groups
    me = lax.axis_index("ctx")
    right, left = me + 1, me - 1

    barrier = pltpu.get_barrier_semaphore()
    for step in range(1, n):
        pl.semaphore_signal(
            barrier, inc=1, device_id={"ctx": lax.rem(me + step, n)}, device_id_type=MESH
        )
    pl.semaphore_wait(barrier, n - 1)

    def shard_copy(hop, part):
        if part == ARRAYS:
            src = own_rows if hop == 1 else halo_rows.at[hop - 2]
            dst = halo_rows.at[hop - 1]
        else:
            src = pack_ref.at[part] if hop == 1 else halo.at[hop - 2, part]
            dst = halo.at[hop - 1, part]
        return pltpu.make_async_remote_copy(
            src_ref=src, dst_ref=dst,
            send_sem=halo_send.at[hop - 1, part], recv_sem=halo_recv.at[hop - 1, part],
            device_id={"ctx": right}, device_id_type=MESH,
        )

    def sends(hop):
        return (me - (hop - 1) >= 0) & (right < n)

    def send_shard(hop, part):
        @pl.when(sends(hop))
        def _():
            shard_copy(hop, part).start()

    def take_shard(hop, part):
        @pl.when(me - hop >= 0)
        def _():
            shard_copy(hop, part).wait_recv()

    for part in range(ARRAYS):
        send_shard(1, part)

    for hop in range(1, reach + 1):
        @pl.when(me - hop < 0)
        def _():
            halo[hop - 1] = jnp.zeros(halo.shape[1:], halo.dtype)
            halo_rows[hop - 1] = jnp.zeros(halo_rows.shape[1:], F32)

    @pl.when(me == n - 1)
    def _():
        recv_back[...] = jnp.zeros(recv_back.shape, recv_back.dtype)

    pos_row = pos_ref[...].astype(F32)
    pos_last = pos_row[:, tokens - 1 :]
    token_row = lax.broadcasted_iota(jnp.int32, (1, tokens), 1).astype(F32)
    row_id = lax.broadcasted_iota(jnp.int32, (tokens, tokens), 0)
    col_id = lax.broadcasted_iota(jnp.int32, (tokens, tokens), 1)
    upper = jnp.where(row_id <= col_id, 1.0, 0.0).astype(F32)
    level[...] = lax.dot_general(
        decay_ref[...], upper, (((0,), (0,)), ((), ())),
        precision=lax.Precision.HIGHEST, preferred_element_type=F32,
    )
    levels = level[...]
    last = levels[:, tokens - 1 :]
    own_tail[...] = jnp.where(
        token_row >= tokens - 1 - pos_last, jnp.exp(last - levels), 0.0
    )
    own_decay[...] = jnp.broadcast_to(
        jnp.where(pos_last > tokens - 1, jnp.exp(last), 0.0), (heads, LANES)
    )
    own_rows[:, :tokens] = own_tail[...]
    own_rows[:, tokens:] = own_decay[...]
    send_shard(1, ARRAYS)
    head_rows[...] = jnp.where(pos_row > token_row, jnp.exp(levels), 0.0)
    pos_col = column_of(pos_row)
    pos_wide = wide(pos_col, tokens)
    apart = (row_id - col_id).astype(F32)
    bias[0] = jnp.where((apart >= 0) & (apart <= pos_wide), 0.0, HIDDEN)
    for hop in range(1, reach + 1):
        bias[hop] = jnp.where(apart + hop * tokens <= pos_wide, 0.0, HIDDEN)
    head_mask = pos_col > lax.broadcasted_iota(jnp.int32, (tokens, LANES), 0).astype(F32)
    head_mask = jnp.where(head_mask, 1.0, 0.0)
    for g in range(groups):
        write_t[g] = jnp.zeros(write_t.shape[1:], F32)
        input_t[g] = jnp.zeros(input_t.shape[1:], F32)
    score_scale = math.log2(math.e) / math.sqrt(width)

    def local_part(h, _):
        g = h // repeat
        c = c_ref[h]
        level_row = level[pl.ds(h, 1), :]
        level_col = column_of(level_row)
        head_col[h] = jnp.exp(level_col) * head_mask
        faded = jnp.exp(wide(level_col, tokens) - level_row + bias[0])
        fade[h] = faded
        within = (faded * nt(c, pack_ref[WRITE, g])).astype(BF16)
        kern[h] = within
        intra[h] = nn(within, pack_ref[INPUT, g])
        scores = nt(q_ref[h], pack_ref[KEY, g]) * score_scale + bias[0]
        top = jnp.max(scores, axis=1, keepdims=True)
        weights = jnp.exp2(scores - top).astype(BF16)
        accum[h] = nn(weights, pack_ref[VALUE, g])
        best[h] = jnp.broadcast_to(top, (tokens, LANES))
        c_t[h] = c.T
        return 0

    lax.fori_loop(0, heads, local_part, 0)

    for hop in range(1, reach + 1):
        for part in range(ARRAYS + 1):
            take_shard(hop, part)
            if hop < reach:
                send_shard(hop + 1, part)
    running = jnp.ones((heads, 1), F32)
    for hop in range(1, reach + 1):
        faded_tail[hop - 1] = halo_rows[hop - 1, :, :tokens] * running
        running = running * halo_rows[hop - 1, :, tokens : tokens + 1]
        for g in range(groups):
            halo_wt[hop - 1, g] = halo[hop - 1, WRITE, g].T

    def back_copy(h):
        return pltpu.make_async_remote_copy(
            src_ref=send_back.at[h], dst_ref=recv_back.at[h],
            send_sem=back_send.at[h], recv_sem=back_recv.at[h],
            device_id={"ctx": left}, device_id_type=MESH,
        )

    def chain(h):
        @pl.when(me < n - 1)
        def _():
            back_copy(h).wait_recv()

        @pl.when(me > 0)
        def _():
            block_decay = own_decay[pl.ds(h, 1), :]
            send_back[h] = (own_back[h] + block_decay * recv_back[h].astype(F32)).astype(BF16)
            back_copy(h).start()

    def main_part(h, _):
        g = h // repeat
        q = q_ref[h]
        c = c_ref[h]
        gain = gain_ref[pl.ds(h, 1), :]
        scores = [
            nt(q, halo[hop, KEY, g]) * score_scale + bias[hop + 1] for hop in range(reach)
        ]
        old_top = best[h]
        top = functools.reduce(jnp.maximum, scores)
        top = jnp.maximum(jnp.max(top, axis=1, keepdims=True), old_top)
        total = accum[h] * jnp.exp2(old_top - top)
        for hop in range(reach):
            weights = jnp.exp2(scores[hop] - wide(top, tokens)).astype(BF16)
            total += nn(weights, halo[hop, VALUE, g])
        target = total * lax.rsqrt(jnp.mean(total * total, axis=1, keepdims=True) + EPSILON)
        target = target.astype(BF16).astype(F32)
        carry = jnp.zeros((c.shape[1], width), F32)
        for hop in range(reach):
            scaled = halo_wt[hop, g].astype(F32) * faded_tail[hop, pl.ds(h, 1), :]
            carry += nn(scaled.astype(BF16), halo[hop, INPUT, g])
        carry_low = carry.astype(BF16)
        head_fade = head_col[h]
        mixer = intra[h] + head_fade * nn(c, carry_low)
        inverse = lax.rsqrt(jnp.mean(mixer * mixer, axis=1, keepdims=True) + STUDENT_FLOOR)
        normed = mixer * inverse
        residual = normed * gain - target
        gain_sum[pl.ds(h, 1), :] = jnp.sum(residual * normed, axis=0, keepdims=True)
        slope = residual * gain
        slope = (slope - normed * jnp.mean(slope * normed, axis=1, keepdims=True)) * inverse
        grad = slope.astype(BF16)
        faded_c = (c_t[h].astype(F32) * head_rows[pl.ds(h, 1), :]).astype(BF16)
        own_back[h] = nn(faded_c, grad)
        grad_kernel = (fade[h] * nt(grad, pack_ref[INPUT, g])).astype(BF16)
        readout = nn(grad_kernel, pack_ref[WRITE, g]) + head_fade * nt(grad, carry_low)
        readout_ref[h] = readout.astype(BF16)
        write_t[g] += nn(c_t[h], grad_kernel)
        input_t[g] += nn(grad.T, kern[h])

        @pl.when(h > 0)
        def _():
            chain(h - 1)

        return 0

    lax.fori_loop(0, heads, main_part, 0)
    chain(heads - 1)

    def gain_copy(step):
        return pltpu.make_async_remote_copy(
            src_ref=gain_sum, dst_ref=gain_slots.at[step - 1],
            send_sem=gain_send.at[step - 1], recv_sem=gain_recv.at[step - 1],
            device_id={"ctx": lax.rem(me + step, n)}, device_id_type=MESH,
        )

    for step in range(1, n):
        gain_copy(step).start()

    def tail_part(h, _):
        g = h // repeat
        tail = own_tail[pl.ds(h, 1), :]
        back = recv_back[h]
        write_t[g] += tail * nt(back, pack_ref[INPUT, g])
        input_t[g] += tail * nt(back.T, pack_ref[WRITE, g])
        return 0

    lax.fori_loop(0, heads, tail_part, 0)
    for g in range(groups):
        write_ref[g] = write_t[g].T.astype(BF16)
        input_ref[g] = input_t[g].T.astype(BF16)

    total_gain = gain_sum[...]
    for step in range(1, n):
        gain_copy(step).wait_recv()
        total_gain += gain_slots[step - 1]
    gain_out_ref[...] = total_gain * (1.0 / (tokens * n))
    for step in range(1, n):
        gain_copy(step).wait_send()
    for hop in range(1, reach + 1):
        @pl.when(sends(hop))
        def _():
            for part in range(ARRAYS + 1):
                shard_copy(hop, part).wait_send()

    @pl.when(me > 0)
    def _():
        def drain(h, _):
            back_copy(h).wait_send()
            return 0

        lax.fori_loop(0, heads, drain, 0)


def body(queries, keys, values, doc_pos, log_decay, student_c, student_write, student_input, gain):
    tokens, heads, width = queries.shape
    groups = keys.shape[1]
    state = student_c.shape[2]
    n = lax.axis_size("ctx")
    reach = max(1, n // 2)
    pack = jnp.stack([student_write, student_input, keys, values]).transpose(0, 2, 1, 3)
    vmem = pl.BlockSpec(memory_space=pltpu.VMEM)
    rows = tokens + LANES
    readout, write, inputs, gain_grad = pl.pallas_call(
        functools.partial(kernel, n, reach),
        out_shape=(
            jax.ShapeDtypeStruct((heads, tokens, state), BF16),
            jax.ShapeDtypeStruct((groups, tokens, state), BF16),
            jax.ShapeDtypeStruct((groups, tokens, width), BF16),
            jax.ShapeDtypeStruct((heads, width), F32),
        ),
        in_specs=[vmem] * 6,
        out_specs=(vmem,) * 4,
        scratch_shapes=[
            pltpu.VMEM((reach, ARRAYS, groups, tokens, width), BF16),
            pltpu.VMEM((heads, tokens), F32),
            pltpu.VMEM((heads, LANES), F32),
            pltpu.VMEM((heads, rows), F32),
            pltpu.VMEM((reach, heads, rows), F32),
            pltpu.VMEM((heads, tokens), F32),
            pltpu.VMEM((heads, tokens), F32),
            pltpu.VMEM((reach, heads, tokens), F32),
            pltpu.VMEM((reach, groups, state, tokens), BF16),
            pltpu.VMEM((heads, state, tokens), BF16),
            pltpu.VMEM((heads, tokens, tokens), F32),
            pltpu.VMEM((heads, tokens, tokens), BF16),
            pltpu.VMEM((heads, tokens, width), F32),
            pltpu.VMEM((heads, tokens, width), F32),
            pltpu.VMEM((heads, tokens, LANES), F32),
            pltpu.VMEM((heads, tokens, LANES), F32),
            pltpu.VMEM((reach + 1, tokens, tokens), F32),
            pltpu.VMEM((heads, state, width), F32),
            pltpu.VMEM((heads, state, width), BF16),
            pltpu.VMEM((heads, state, width), BF16),
            pltpu.VMEM((groups, state, tokens), F32),
            pltpu.VMEM((groups, width, tokens), F32),
            pltpu.VMEM((heads, width), F32),
            pltpu.VMEM((n - 1, heads, width), F32),
            pltpu.SemaphoreType.DMA((reach, ARRAYS + 1)),
            pltpu.SemaphoreType.DMA((reach, ARRAYS + 1)),
            pltpu.SemaphoreType.DMA((heads,)),
            pltpu.SemaphoreType.DMA((heads,)),
            pltpu.SemaphoreType.DMA((n - 1,)),
            pltpu.SemaphoreType.DMA((n - 1,)),
        ],
        compiler_params=pltpu.CompilerParams(
            collective_id=0, has_side_effects=True, vmem_limit_bytes=48 * 2**20
        ),
    )(
        queries.transpose(1, 0, 2),
        student_c.transpose(1, 0, 2),
        pack,
        log_decay,
        doc_pos.reshape(1, tokens),
        gain,
    )
    return (
        readout.transpose(1, 0, 2),
        write.transpose(1, 0, 2),
        inputs.transpose(1, 0, 2),
        gain_grad,
    )


def solution(mesh):
    tokens = P(("groups", "ctx"), "tp", None)
    return jax.shard_map(
        body,
        mesh=mesh,
        in_specs=(
            tokens, tokens, tokens, P(("groups", "ctx")), P(("groups", "ctx"), "tp"),
            tokens, tokens, tokens, P("tp", None),
        ),
        out_specs=(tokens, tokens, tokens, P(("groups", "tp"), None)),
        check_vma=False,
    )
```

time: 226 us -> 72.1 us (0.32)
  blocking collectives: 72 us -> 0 us
  waiting for transfers between devices: 69.2 us -> 0 us
  Pallas kernels: 0 us -> 63 us
  matrix products: 25.4 us -> 0 us
  other arithmetic: 15.9 us -> 0.07 us
  local copies, waits for them, and re-layouts: 23.8 us -> 8.06 us
  between operations: 15.1 us -> 0.7 us
  loops' own time: 3.88 us -> 0 us
    all_gather x2 -> x0, waiting for transfers between devices: 69.1 us -> none  [entering(): pieces = jax.tree.map(lambda part: lax.all_gather(part, axis), value)]
    pallas_call x0 -> x1, Pallas kernels: none -> 63 us  [body(): pl.pallas_call(functools.partial(kernel, n, reach), out_shape=(jax.ShapeD...]
    all_gather x3 -> x0, blocking collectives: 60.2 us -> none  [the longest x1 24.2 us: body(): lax.all_gather(keys, 'ctx', axis=0, tiled=True)]
    dot_general x14 -> x0, matrix products: 25.4 us -> none  [the longest x1 3.12 us: body(): jnp.einsum('thp,hnp->thn', mixer_grad, carry_low, preferred_element_type=...]
    psum x1 -> x0, blocking collectives: 11.9 us -> none  [body(): grad_gain = lax.psum(gain_term, 'ctx')]
    select_n x6 -> x0, other arithmetic: 8.83 us -> none  [step(): jnp.where(position < mine, new, old)]
    unnamed x37 -> x15, local copies, waits for them, and re-layouts: 10.3 us -> 5.43 us
    rev x2 -> x0, local copies, waits for them, and re-layouts: 4.68 us -> none  [entering(): pieces = jax.tree.map(lambda part: part[::-1], pieces)]
  transfers between devices with their start and end apart: 2 -> 0, of which waited for: 2 -> 0; matrix products, arithmetic and copies ran while one was open for 13% -> 0% of each run, Pallas kernels for 0% -> 0%
where the time goes in v1:
time: 72.1 us; the launch traced here: 71.8 us
  Pallas kernels  63 us (87%)
  local copies, waits for them, and re-layouts  8.06 us (11%)
    pallas_call x1, Pallas kernels, body(): pl.pallas_call(functools.partial(kernel, n, reach), out_shape=(jax.ShapeD...  63 us
    unnamed x15, local copies, waits for them, and re-layouts  5.43 us
    another operation x2, local copies, waits for them, and re-layouts, body(): jnp.stack([student_write, student_input, keys, values])  2.09 us

profile of v1, /device:TPU:0, one launch (start us, length us, event | category | flops | bytes accessed | tf_op | source)
XLA Modules:
  0.0 71.8 jit_solution(9337366136399461627)
XLA Ops:
  0.6 0.0 copy-start.4
  0.6 0.9 %copy.19.decay_ref = f32[256,16]{1,0:T(8,128)S(1)} copy(f32[256,16]{0,1:T(8,128)} %param.13) | data formatting | bytes 32768 | tf_op args[4]
  1.5 0.1 copy-done.4
  1.6 0.0 copy-start.2
  1.6 0.0 copy-start.3
  1.6 1.1 %copy_bitcast_fusion.2 = (bf16[1,256,2,128]{3,1,2,0:T(8,128)(2,1)S(1)}, bf16[1,256,2,128]{3,1,2,0:T(8,128)(2,1)S(1)}) fusion(bf16[256,2,128]{2,1,0:T(2,128)(2,1)S(1)} %copy-done.4, bf16[256,2,128]{2,1,0:T(2,128)(2,1)} %param.10), kind=kLoop, calls=%fused_computation.3 | loop fusion | bytes 524288 | tf_op jit(solution)/shard_map/stack | solution.py:284
  2.6 1.0 %copy_bitcast_fusion.4 = (bf16[1,256,2,128]{3,1,2,0:T(8,128)(2,1)S(1)}, bf16[1,256,2,128]{3,1,2,0:T(8,128)(2,1)S(1)}) fusion(bf16[256,2,128]{2,1,0:T(2,128)(2,1)} %param.16, bf16[256,2,128]{2,1,0:T(2,128)(2,1)} %param.15), kind=kLoop, calls=%fused_computation.5 | loop fusion | bytes 524288 | tf_op jit(solution)/shard_map/stack | solution.py:284
  3.7 0.1 maximum_bitcast_fusion.pack_ref
  3.7 0.0 copy-done.2
  3.7 0.0 copy-done.3
  3.8 0.0 copy-start
  3.8 0.5 copy_bitcast_fusion
  4.3 0.0 copy-start.1
  4.3 0.1 copy-done
  4.5 0.5 copy-done.1
  5.0 63.0 %shard_map.120 = (bf16[16,256,128]{2,1,0:T(8,128)(2,1)S(1)}, bf16[2,256,128]{2,1,0:T(8,128)(2,1)S(1)}, bf16[2,256,128]{2,1,0:T(8,128)(2,1)S(1)}, f32[16,128]{1,0:T(8,128)S(1)}) custom-call(bf16[16,256,128]{2,1,0:T(8,128)(2,1)S(1)} %get-tuple-element.21.q_ref, bf16[16,256,128]{2,1,0:T(8,128)(2,1)S(1)} %get-tuple-element.20.c_ref, ...), custom_call_target="tpu_custom_call" | custom-call | tf_op jit(solution)/shard_map/pallas_call | solution.py:287
  68.0 1.6 %copy.20 = bf16[256,16,128]{2,1,0:T(8,128)(2,1)} copy(bf16[256,16,128]{2,0,1:T(8,128)(2,1)S(1)} %bitcast.18) | data formatting | bytes 2097152
  69.6 0.8 %copy.21 = bf16[256,2,128]{2,1,0:T(2,128)(2,1)} copy(bf16[256,2,128]{2,0,1:T(8,128)(2,1)S(1)} %bitcast.20) | data formatting | bytes 262144
  70.4 0.8 %copy.22 = bf16[256,2,128]{2,1,0:T(2,128)(2,1)} copy(bf16[256,2,128]{2,0,1:T(8,128)(2,1)S(1)} %bitcast.19) | data formatting | bytes 262144
  71.2 0.6 copy.30
Async XLA Ops:
  0.6 0.9 %copy-start.4 = (bf16[256,2,128]{2,1,0:T(2,128)(2,1)S(1)}, bf16[256,2,128]{2,1,0:T(2,128)(2,1)}, u32[]{:S(2)}) copy-start(bf16[256,2,128]{2,1,0:T(2,128)(2,1)} %param.11) | copy-start | bytes 393220
  1.6 2.2 %copy-start.2 = (bf16[256,16,128]{2,1,0:T(8,128)(2,1)S(1)}, bf16[256,16,128]{2,1,0:T(8,128)(2,1)}, u32[]{:S(2)}) copy-start(bf16[256,16,128]{2,1,0:T(8,128)(2,1)} %param.14) | copy-start | bytes 3145732
  1.6 2.2 %copy-start.3 = (bf16[256,16,128]{2,1,0:T(8,128)(2,1)S(1)}, bf16[256,16,128]{2,1,0:T(8,128)(2,1)}, u32[]{:S(2)}) copy-start(bf16[256,16,128]{2,1,0:T(8,128)(2,1)} %param.9) | copy-start | bytes 3145732
  3.8 0.7 copy-start
  4.3 0.7 copy-start.1

commit v2 on v1

--- a/solution.py
+++ b/solution.py
@@ -17,6 +17,7 @@
 MESH = pl.DeviceIdType.MESH
 WRITE, INPUT, KEY, VALUE = range(4)
 ARRAYS = 4
+TOGETHER = 4
 
 
 def nn(a, b):
@@ -45,7 +46,7 @@
     halo_send, halo_recv, back_send, back_recv, gain_send, gain_recv,
 ):
     heads, tokens, width = q_ref.shape
-    groups = pack_ref.shape[1]
+    groups = pack_ref.shape[0]
     repeat = heads // groups
     me = lax.axis_index("ctx")
     right, left = me + 1, me - 1
@@ -58,7 +59,7 @@
     pl.semaphore_wait(barrier, n - 1)
 
     def shard_copy(hop, part):
-        if part == ARRAYS:
+        if part == groups:
             src = own_rows if hop == 1 else halo_rows.at[hop - 2]
             dst = halo_rows.at[hop - 1]
         else:
@@ -83,8 +84,7 @@
         def _():
             shard_copy(hop, part).wait_recv()
 
-    for part in range(ARRAYS):
-        send_shard(1, part)
+    send_shard(1, 0)
 
     for hop in range(1, reach + 1):
         @pl.when(me - hop < 0)
@@ -102,9 +102,8 @@
     row_id = lax.broadcasted_iota(jnp.int32, (tokens, tokens), 0)
     col_id = lax.broadcasted_iota(jnp.int32, (tokens, tokens), 1)
     upper = jnp.where(row_id <= col_id, 1.0, 0.0).astype(F32)
-    level[...] = lax.dot_general(
-        decay_ref[...], upper, (((0,), (0,)), ((), ())),
-        precision=lax.Precision.HIGHEST, preferred_element_type=F32,
+    level[...] = jnp.dot(
+        decay_ref[...], upper, precision=lax.Precision.HIGHEST, preferred_element_type=F32
     )
     levels = level[...]
     last = levels[:, tokens - 1 :]
@@ -116,7 +115,7 @@
     )
     own_rows[:, :tokens] = own_tail[...]
     own_rows[:, tokens:] = own_decay[...]
-    send_shard(1, ARRAYS)
+    send_shard(1, groups)
     head_rows[...] = jnp.where(pos_row > token_row, jnp.exp(levels), 0.0)
     pos_col = column_of(pos_row)
     pos_wide = wide(pos_col, tokens)
@@ -131,7 +130,7 @@
         input_t[g] = jnp.zeros(input_t.shape[1:], F32)
     score_scale = math.log2(math.e) / math.sqrt(width)
 
-    def local_part(h, _):
+    def local_part(h):
         g = h // repeat
         c = c_ref[h]
         level_row = level[pl.ds(h, 1), :]
@@ -139,30 +138,53 @@
         head_col[h] = jnp.exp(level_col) * head_mask
         faded = jnp.exp(wide(level_col, tokens) - level_row + bias[0])
         fade[h] = faded
-        within = (faded * nt(c, pack_ref[WRITE, g])).astype(BF16)
+        within = (faded * nt(c, pack_ref[g, WRITE])).astype(BF16)
         kern[h] = within
-        intra[h] = nn(within, pack_ref[INPUT, g])
-        scores = nt(q_ref[h], pack_ref[KEY, g]) * score_scale + bias[0]
+        intra[h] = nn(within, pack_ref[g, INPUT])
+        scores = nt(q_ref[h], pack_ref[g, KEY]) * score_scale + bias[0]
         top = jnp.max(scores, axis=1, keepdims=True)
         weights = jnp.exp2(scores - top).astype(BF16)
-        accum[h] = nn(weights, pack_ref[VALUE, g])
+        accum[h] = nn(weights, pack_ref[g, VALUE])
         best[h] = jnp.broadcast_to(top, (tokens, LANES))
         c_t[h] = c.T
-        return 0
-
-    lax.fori_loop(0, heads, local_part, 0)
-
-    for hop in range(1, reach + 1):
-        for part in range(ARRAYS + 1):
+
+    def arrive(group, hop):
+        parts = (group, groups) if group == 0 else (group,)
+        for part in parts:
             take_shard(hop, part)
             if hop < reach:
                 send_shard(hop + 1, part)
-    running = jnp.ones((heads, 1), F32)
-    for hop in range(1, reach + 1):
-        faded_tail[hop - 1] = halo_rows[hop - 1, :, :tokens] * running
-        running = running * halo_rows[hop - 1, :, tokens : tokens + 1]
-        for g in range(groups):
-            halo_wt[hop - 1, g] = halo[hop - 1, WRITE, g].T
+        if hop == 1 and group + 1 < groups:
+            send_shard(1, group + 1)
+
+    def ready(group):
+        for hop in range(2, reach + 1):
+            arrive(group, hop)
+        if group == 0:
+            running = jnp.ones((heads, 1), F32)
+            for hop in range(1, reach + 1):
+                faded_tail[hop - 1] = halo_rows[hop - 1, :, :tokens] * running
+                running = running * halo_rows[hop - 1, :, tokens : tokens + 1]
+        for hop in range(1, reach + 1):
+            halo_wt[hop - 1, group] = halo[hop - 1, group, WRITE].T
+
+    together = math.gcd(repeat, TOGETHER)
+
+    def per_heads(first, past, part, after=None):
+        def step(index, _):
+            for offset in range(together):
+                part(index * together + offset)
+            if after is not None:
+                after(index)
+            return 0
+
+        lax.fori_loop(first // together, past // together, step, 0)
+
+    per_heads(0, repeat, local_part)
+    arrive(0, 1)
+    if groups > 1:
+        per_heads(repeat, heads, local_part)
+    ready(0)
 
     def back_copy(h):
         return pltpu.make_async_remote_copy(
@@ -182,13 +204,13 @@
             send_back[h] = (own_back[h] + block_decay * recv_back[h].astype(F32)).astype(BF16)
             back_copy(h).start()
 
-    def main_part(h, _):
+    def main_part(h):
         g = h // repeat
         q = q_ref[h]
         c = c_ref[h]
         gain = gain_ref[pl.ds(h, 1), :]
         scores = [
-            nt(q, halo[hop, KEY, g]) * score_scale + bias[hop + 1] for hop in range(reach)
+            nt(q, halo[hop, g, KEY]) * score_scale + bias[hop + 1] for hop in range(reach)
         ]
         old_top = best[h]
         top = functools.reduce(jnp.maximum, scores)
@@ -196,13 +218,13 @@
         total = accum[h] * jnp.exp2(old_top - top)
         for hop in range(reach):
             weights = jnp.exp2(scores[hop] - wide(top, tokens)).astype(BF16)
-            total += nn(weights, halo[hop, VALUE, g])
+            total += nn(weights, halo[hop, g, VALUE])
         target = total * lax.rsqrt(jnp.mean(total * total, axis=1, keepdims=True) + EPSILON)
         target = target.astype(BF16).astype(F32)
         carry = jnp.zeros((c.shape[1], width), F32)
         for hop in range(reach):
             scaled = halo_wt[hop, g].astype(F32) * faded_tail[hop, pl.ds(h, 1), :]
-            carry += nn(scaled.astype(BF16), halo[hop, INPUT, g])
+            carry += nn(scaled.astype(BF16), halo[hop, g, INPUT])
         carry_low = carry.astype(BF16)
         head_fade = head_col[h]
         mixer = intra[h] + head_fade * nn(c, carry_low)
@@ -215,20 +237,34 @@
         grad = slope.astype(BF16)
         faded_c = (c_t[h].astype(F32) * head_rows[pl.ds(h, 1), :]).astype(BF16)
         own_back[h] = nn(faded_c, grad)
-        grad_kernel = (fade[h] * nt(grad, pack_ref[INPUT, g])).astype(BF16)
-        readout = nn(grad_kernel, pack_ref[WRITE, g]) + head_fade * nt(grad, carry_low)
+        grad_kernel = (fade[h] * nt(grad, pack_ref[g, INPUT])).astype(BF16)
+        readout = nn(grad_kernel, pack_ref[g, WRITE]) + head_fade * nt(grad, carry_low)
         readout_ref[h] = readout.astype(BF16)
         write_t[g] += nn(c_t[h], grad_kernel)
         input_t[g] += nn(grad.T, kern[h])
 
-        @pl.when(h > 0)
-        def _():
-            chain(h - 1)
-
-        return 0
-
-    lax.fori_loop(0, heads, main_part, 0)
-    chain(heads - 1)
+    behind = n - 1 - me
+    steps = heads // together
+
+    def hand_on(index):
+        for offset in range(together):
+            chain(index * together + offset)
+
+    def hand_on_late(index):
+        @pl.when(index - behind >= 0)
+        def _():
+            hand_on(index - behind)
+
+    half = repeat // together // 2 * together
+    for group in range(groups):
+        first = group * repeat
+        if group + 1 < groups:
+            per_heads(first, first + half, main_part, hand_on_late)
+            arrive(group + 1, 1)
+            per_heads(first + half, first + repeat, main_part, hand_on_late)
+            ready(group + 1)
+        else:
+            per_heads(first, first + repeat, main_part, hand_on_late)
 
     def gain_copy(step):
         return pltpu.make_async_remote_copy(
@@ -240,15 +276,23 @@
     for step in range(1, n):
         gain_copy(step).start()
 
-    def tail_part(h, _):
+    def tail_part(h):
         g = h // repeat
         tail = own_tail[pl.ds(h, 1), :]
         back = recv_back[h]
-        write_t[g] += tail * nt(back, pack_ref[INPUT, g])
-        input_t[g] += tail * nt(back.T, pack_ref[WRITE, g])
+        write_t[g] += tail * nt(back, pack_ref[g, INPUT])
+        input_t[g] += tail * nt(back.T, pack_ref[g, WRITE])
+
+    def tail_step(index, _):
+        @pl.when(index + behind >= steps)
+        def _():
+            hand_on(index)
+
+        for offset in range(together):
+            tail_part(index * together + offset)
         return 0
 
-    lax.fori_loop(0, heads, tail_part, 0)
+    lax.fori_loop(0, steps, tail_step, 0)
     for g in range(groups):
         write_ref[g] = write_t[g].T.astype(BF16)
         input_ref[g] = input_t[g].T.astype(BF16)
@@ -263,7 +307,7 @@
     for hop in range(1, reach + 1):
         @pl.when(sends(hop))
         def _():
-            for part in range(ARRAYS + 1):
+            for part in range(groups + 1):
                 shard_copy(hop, part).wait_send()
 
     @pl.when(me > 0)
@@ -281,7 +325,7 @@
     state = student_c.shape[2]
     n = lax.axis_size("ctx")
     reach = max(1, n // 2)
-    pack = jnp.stack([student_write, student_input, keys, values]).transpose(0, 2, 1, 3)
+    pack = jnp.stack([student_write, student_input, keys, values]).transpose(2, 0, 1, 3)
     vmem = pl.BlockSpec(memory_space=pltpu.VMEM)
     rows = tokens + LANES
     readout, write, inputs, gain_grad = pl.pallas_call(
@@ -295,7 +339,7 @@
         in_specs=[vmem] * 6,
         out_specs=(vmem,) * 4,
         scratch_shapes=[
-            pltpu.VMEM((reach, ARRAYS, groups, tokens, width), BF16),
+            pltpu.VMEM((reach, groups, ARRAYS, tokens, width), BF16),
             pltpu.VMEM((heads, tokens), F32),
             pltpu.VMEM((heads, LANES), F32),
             pltpu.VMEM((heads, rows), F32),
@@ -319,8 +363,8 @@
             pltpu.VMEM((groups, width, tokens), F32),
             pltpu.VMEM((heads, width), F32),
             pltpu.VMEM((n - 1, heads, width), F32),
-            pltpu.SemaphoreType.DMA((reach, ARRAYS + 1)),
-            pltpu.SemaphoreType.DMA((reach, ARRAYS + 1)),
+            pltpu.SemaphoreType.DMA((reach, groups + 1)),
+            pltpu.SemaphoreType.DMA((reach, groups + 1)),
             pltpu.SemaphoreType.DMA((heads,)),
             pltpu.SemaphoreType.DMA((heads,)),
             pltpu.SemaphoreType.DMA((n - 1,)),
@@ -333,7 +377,7 @@
         queries.transpose(1, 0, 2),
         student_c.transpose(1, 0, 2),
         pack,
-        log_decay,
+        log_decay.T,
         doc_pos.reshape(1, tokens),
         gain,
     )

time: 72.1 us -> 60.6 us (0.84)
  Pallas kernels: 63 us -> 52.4 us
  local copies, waits for them, and re-layouts: 8.06 us -> 7.22 us
    pallas_call x1, Pallas kernels: 63 us -> 52.4 us  [body(): pl.pallas_call(functools.partial(kernel, n, reach), out_shape=(jax.ShapeD...]
    unnamed x15 -> x14, local copies, waits for them, and re-layouts: 5.43 us -> 4.52 us
where the time goes in v2:
time: 60.6 us; the launch traced here: 60.4 us
  Pallas kernels  52.4 us (86%)
  local copies, waits for them, and re-layouts  7.22 us (12%)
  between operations  0.72 us (1%)
    pallas_call x1, Pallas kernels, body(): pl.pallas_call(functools.partial(kernel, n, reach), out_shape=(jax.ShapeD...  52.4 us
    unnamed x14, local copies, waits for them, and re-layouts  4.52 us
    another operation x2, local copies, waits for them, and re-layouts, body(): jnp.stack([student_write, student_input, keys, values])  2.16 us

profile of v2, /device:TPU:0, one launch (start us, length us, event | category | flops | bytes accessed | tf_op | source)
XLA Modules:
  0.0 60.4 jit_solution(18307463571941856979)
XLA Ops:
  0.6 0.0 copy-start.3
  0.6 0.0 copy-start.4
  0.7 1.1 %copy_bitcast_fusion.2 = (bf16[1,256,2,128]{3,1,0,2:T(8,128)(2,1)S(1)}, bf16[1,256,2,128]{3,1,0,2:T(8,128)(2,1)S(1)}) fusion(bf16[256,2,128]{2,1,0:T(2,128)(2,1)} %param.11, bf16[256,2,128]{2,1,0:T(2,128)(2,1)} %param.10), kind=kLoop, calls=%fused_computation.3 | loop fusion | bytes 524288 | tf_op jit(solution)/shard_map/stack | solution.py:328
  1.8 1.0 %copy_bitcast_fusion.4 = (bf16[1,256,2,128]{3,1,0,2:T(8,128)(2,1)S(1)}, bf16[1,256,2,128]{3,1,0,2:T(8,128)(2,1)S(1)}) fusion(bf16[256,2,128]{2,1,0:T(2,128)(2,1)} %param.16, bf16[256,2,128]{2,1,0:T(2,128)(2,1)} %param.15), kind=kLoop, calls=%fused_computation.5 | loop fusion | bytes 524288 | tf_op jit(solution)/shard_map/stack | solution.py:328
  2.8 0.1 maximum_bitcast_fusion.pack_ref
  2.9 0.0 copy-done.3
  2.9 0.0 copy-done.4
  2.9 0.0 copy-start
  2.9 0.0 copy-start.1
  2.9 0.5 copy_bitcast_fusion
  3.5 0.0 copy-start.2
  3.5 0.1 copy-done
  3.6 0.0 copy-done.1
  3.6 0.5 copy-done.2
  4.2 52.4 %shard_map.120 = (bf16[16,256,128]{2,1,0:T(8,128)(2,1)S(1)}, bf16[2,256,128]{2,1,0:T(8,128)(2,1)S(1)}, bf16[2,256,128]{2,1,0:T(8,128)(2,1)S(1)}, f32[16,128]{1,0:T(8,128)S(1)}) custom-call(bf16[16,256,128]{2,1,0:T(8,128)(2,1)S(1)} %get-tuple-element.21.q_ref, bf16[16,256,128]{2,1,0:T(8,128)(2,1)S(1)} %get-tuple-element.20.c_ref, ...), custom_call_target="tpu_custom_call" | custom-call | tf_op jit(solution)/shard_map/pallas_call | solution.py:331
  56.5 1.6 %copy.19 = bf16[256,16,128]{2,1,0:T(8,128)(2,1)} copy(bf16[256,16,128]{2,0,1:T(8,128)(2,1)S(1)} %bitcast.19) | data formatting | bytes 2097152
  58.2 0.8 %copy.20 = bf16[256,2,128]{2,1,0:T(2,128)(2,1)} copy(bf16[256,2,128]{2,0,1:T(8,128)(2,1)S(1)} %bitcast.21) | data formatting | bytes 262144
  59.0 0.8 %copy.21 = bf16[256,2,128]{2,1,0:T(2,128)(2,1)} copy(bf16[256,2,128]{2,0,1:T(8,128)(2,1)S(1)} %bitcast.20) | data formatting | bytes 262144
  59.8 0.6 copy.29
Async XLA Ops:
  0.6 2.3 %copy-start.3 = (bf16[256,16,128]{2,1,0:T(8,128)(2,1)S(1)}, bf16[256,16,128]{2,1,0:T(8,128)(2,1)}, u32[]{:S(2)}) copy-start(bf16[256,16,128]{2,1,0:T(8,128)(2,1)} %param.14) | copy-start | bytes 3145732
  0.6 2.3 %copy-start.4 = (bf16[256,16,128]{2,1,0:T(8,128)(2,1)S(1)}, bf16[256,16,128]{2,1,0:T(8,128)(2,1)}, u32[]{:S(2)}) copy-start(bf16[256,16,128]{2,1,0:T(8,128)(2,1)} %param.9) | copy-start | bytes 3145732
  2.9 0.7 %copy-start = (f32[256,16]{0,1:T(8,128)S(1)}, f32[256,16]{0,1:T(8,128)}, u32[]{:S(2)}) copy-start(f32[256,16]{0,1:T(8,128)} %param.13) | copy-start | bytes 49156
  2.9 0.7 %copy-start.1 = (f32[16,128]{1,0:T(8,128)S(1)}, f32[16,128]{1,0:T(8,128)}, u32[]{:S(2)}) copy-start(f32[16,128]{1,0:T(8,128)} %gain_ref.1) | copy-start | bytes 24580
  3.5 0.7 %copy-start.2 = (s32[256]{0:T(256)S(1)}, s32[256]{0:T(256)}, u32[]{:S(2)}) copy-start(s32[256]{0:T(256)} %param.12) | copy-start | bytes 3076

commit v3 on v2

--- a/solution.py
+++ b/solution.py
@@ -18,6 +18,7 @@
 WRITE, INPUT, KEY, VALUE = range(4)
 ARRAYS = 4
 TOGETHER = 4
+CHUNK = 64
 
 
 def nn(a, b):
@@ -38,14 +39,14 @@
 
 def kernel(
     n, reach,
-    q_ref, c_ref, pack_ref, decay_ref, pos_ref, gain_ref,
-    readout_ref, write_ref, input_ref, gain_out_ref,
-    halo, own_tail, own_decay, own_rows, halo_rows, level, head_rows, faded_tail, halo_wt,
+    q_rows, c_rows, pack_ref, decay_ref, pos_ref, gain_ref,
+    readout_rows, write_ref, input_ref, gain_out_ref,
+    q_ref, c_ref, readout_ref, halo, own_tail, own_decay, own_rows, halo_rows, level, head_rows, faded_tail, halo_wt,
     c_t, fade, kern, intra, accum, best, head_col, bias,
     own_back, send_back, recv_back, write_t, input_t, gain_sum, gain_slots,
     halo_send, halo_recv, back_send, back_recv, gain_send, gain_recv,
 ):
-    heads, tokens, width = q_ref.shape
+    tokens, heads, width = q_rows.shape
     groups = pack_ref.shape[0]
     repeat = heads // groups
     me = lax.axis_index("ctx")
@@ -129,6 +130,14 @@
         write_t[g] = jnp.zeros(write_t.shape[1:], F32)
         input_t[g] = jnp.zeros(input_t.shape[1:], F32)
     score_scale = math.log2(math.e) / math.sqrt(width)
+
+    def by_head(index, _):
+        rows = pl.ds(pl.multiple_of(index * CHUNK, CHUNK), CHUNK)
+        q_ref[:, rows, :] = jnp.transpose(q_rows[rows], (1, 0, 2))
+        c_ref[:, rows, :] = jnp.transpose(c_rows[rows], (1, 0, 2))
+        return 0
+
+    lax.fori_loop(0, tokens // CHUNK, by_head, 0)
 
     def local_part(h):
         g = h // repeat
@@ -159,6 +168,7 @@
 
     def ready(group):
         for hop in range(2, reach + 1):
+            per_heads(group * repeat, (group + 1) * repeat, early_part(hop - 1))
             arrive(group, hop)
         if group == 0:
             running = jnp.ones((heads, 1), F32)
@@ -180,12 +190,6 @@
 
         lax.fori_loop(first // together, past // together, step, 0)
 
-    per_heads(0, repeat, local_part)
-    arrive(0, 1)
-    if groups > 1:
-        per_heads(repeat, heads, local_part)
-    ready(0)
-
     def back_copy(h):
         return pltpu.make_async_remote_copy(
             src_ref=send_back.at[h], dst_ref=recv_back.at[h],
@@ -204,21 +208,25 @@
             send_back[h] = (own_back[h] + block_decay * recv_back[h].astype(F32)).astype(BF16)
             back_copy(h).start()
 
+    def attend(h, hop):
+        g = h // repeat
+        scores = nt(q_ref[h], halo[hop - 1, g, KEY]) * score_scale + bias[hop]
+        old_top = best[h]
+        top = jnp.maximum(jnp.max(scores, axis=1, keepdims=True), old_top)
+        weights = jnp.exp2(scores - wide(top, tokens)).astype(BF16)
+        return top, accum[h] * jnp.exp2(old_top - top) + nn(weights, halo[hop - 1, g, VALUE])
+
+    def early_part(hop):
+        def part(h):
+            best[h], accum[h] = attend(h, hop)
+
+        return part
+
     def main_part(h):
         g = h // repeat
-        q = q_ref[h]
         c = c_ref[h]
         gain = gain_ref[pl.ds(h, 1), :]
-        scores = [
-            nt(q, halo[hop, g, KEY]) * score_scale + bias[hop + 1] for hop in range(reach)
-        ]
-        old_top = best[h]
-        top = functools.reduce(jnp.maximum, scores)
-        top = jnp.maximum(jnp.max(top, axis=1, keepdims=True), old_top)
-        total = accum[h] * jnp.exp2(old_top - top)
-        for hop in range(reach):
-            weights = jnp.exp2(scores[hop] - wide(top, tokens)).astype(BF16)
-            total += nn(weights, halo[hop, g, VALUE])
+        total = attend(h, reach)[1]
         target = total * lax.rsqrt(jnp.mean(total * total, axis=1, keepdims=True) + EPSILON)
         target = target.astype(BF16).astype(F32)
         carry = jnp.zeros((c.shape[1], width), F32)
@@ -256,6 +264,11 @@
             hand_on(index - behind)
 
     half = repeat // together // 2 * together
+    per_heads(0, repeat, local_part)
+    arrive(0, 1)
+    if groups > 1:
+        per_heads(repeat, heads, local_part)
+    ready(0)
     for group in range(groups):
         first = group * repeat
         if group + 1 < groups:
@@ -282,6 +295,13 @@
         back = recv_back[h]
         write_t[g] += tail * nt(back, pack_ref[g, INPUT])
         input_t[g] += tail * nt(back.T, pack_ref[g, WRITE])
+
+    def by_token(index, _):
+        rows = pl.ds(pl.multiple_of(index * CHUNK, CHUNK), CHUNK)
+        readout_rows[rows] = jnp.transpose(readout_ref[:, rows, :], (1, 0, 2))
+        return 0
+
+    lax.fori_loop(0, tokens // CHUNK, by_token, 0)
 
     def tail_step(index, _):
         @pl.when(index + behind >= steps)
@@ -331,7 +351,7 @@
     readout, write, inputs, gain_grad = pl.pallas_call(
         functools.partial(kernel, n, reach),
         out_shape=(
-            jax.ShapeDtypeStruct((heads, tokens, state), BF16),
+            jax.ShapeDtypeStruct((tokens, heads, state), BF16),
             jax.ShapeDtypeStruct((groups, tokens, state), BF16),
             jax.ShapeDtypeStruct((groups, tokens, width), BF16),
             jax.ShapeDtypeStruct((heads, width), F32),
@@ -339,6 +359,9 @@
         in_specs=[vmem] * 6,
         out_specs=(vmem,) * 4,
         scratch_shapes=[
+            pltpu.VMEM((heads, tokens, width), BF16),
+            pltpu.VMEM((heads, tokens, state), BF16),
+            pltpu.VMEM((heads, tokens, state), BF16),
             pltpu.VMEM((reach, groups, ARRAYS, tokens, width), BF16),
             pltpu.VMEM((heads, tokens), F32),
             pltpu.VMEM((heads, LANES), F32),
@@ -374,15 +397,15 @@
             collective_id=0, has_side_effects=True, vmem_limit_bytes=48 * 2**20
         ),
     )(
-        queries.transpose(1, 0, 2),
-        student_c.transpose(1, 0, 2),
+        queries,
+        student_c,
         pack,
         log_decay.T,
         doc_pos.reshape(1, tokens),
         gain,
     )
     return (
-        readout.transpose(1, 0, 2),
+        readout,
         write.transpose(1, 0, 2),
         inputs.transpose(1, 0, 2),
         gain_grad,

time: 60.6 us -> 60 us (0.990)
  Pallas kernels: 52.4 us -> 51.6 us
    pallas_call x1, Pallas kernels: 52.4 us -> 51.6 us  [body(): pl.pallas_call(functools.partial(kernel, n, reach), out_shape=(jax.ShapeD...]
    unnamed x14, local copies, waits for them, and re-layouts: 4.52 us -> 5.15 us
where the time goes in v3:
time: 60 us; the launch traced here: 59.6 us
  Pallas kernels  51.6 us (86%)
  local copies, waits for them, and re-layouts  7.3 us (12%)
  between operations  0.7 us (1%)
    pallas_call x1, Pallas kernels, body(): pl.pallas_call(functools.partial(kernel, n, reach), out_shape=(jax.ShapeD...  51.6 us
    unnamed x14, local copies, waits for them, and re-layouts  5.15 us
    another operation x2, local copies, waits for them, and re-layouts, body(): jnp.stack([student_write, student_input, keys, values])  2.16 us

profile of v3, /device:TPU:0, one launch (start us, length us, event | category | flops | bytes accessed | tf_op | source)
XLA Modules:
  0.0 59.6 jit_solution(5374062544824477225)
XLA Ops:
  0.6 0.0 copy-start
  0.6 0.0 copy-start.1
  0.7 1.1 %copy_bitcast_fusion = (bf16[1,256,2,128]{3,1,0,2:T(8,128)(2,1)S(1)}, bf16[1,256,2,128]{3,1,0,2:T(8,128)(2,1)S(1)}) fusion(bf16[256,2,128]{2,1,0:T(2,128)(2,1)} %param.11, bf16[256,2,128]{2,1,0:T(2,128)(2,1)} %param.10), kind=kLoop, calls=%fused_computation.1 | loop fusion | bytes 524288 | tf_op jit(solution)/shard_map/stack | solution.py:348
  1.8 1.0 %copy_bitcast_fusion.2 = (bf16[1,256,2,128]{3,1,0,2:T(8,128)(2,1)S(1)}, bf16[1,256,2,128]{3,1,0,2:T(8,128)(2,1)S(1)}) fusion(bf16[256,2,128]{2,1,0:T(2,128)(2,1)} %param.16, bf16[256,2,128]{2,1,0:T(2,128)(2,1)} %param.15), kind=kLoop, calls=%fused_computation.3 | loop fusion | bytes 524288 | tf_op jit(solution)/shard_map/stack | solution.py:348
  2.8 0.0 copy-start.4
  2.8 0.1 maximum_bitcast_fusion.pack_ref
  2.9 0.0 copy-done
  2.9 0.0 copy-done.1
  2.9 0.6 copy-done.4
  3.5 0.0 copy-start.2
  3.5 0.7 %copy-done.2 = f32[256,16]{0,1:T(8,128)S(1)} copy-done((f32[256,16]{0,1:T(8,128)S(1)}, f32[256,16]{0,1:T(8,128)}, u32[]{:S(2)}) %copy-start.2) | copy-done | bytes 16408
  4.2 0.0 copy-start.3
  4.2 0.7 %copy-done.3 = f32[16,128]{1,0:T(8,128)S(1)} copy-done((f32[16,128]{1,0:T(8,128)S(1)}, f32[16,128]{1,0:T(8,128)}, u32[]{:S(2)}) %copy-start.3) | copy-done | bytes 8216
  4.9 51.6 %shard_map.120 = (bf16[256,16,128]{2,1,0:T(8,128)(2,1)S(1)}, bf16[2,256,128]{2,1,0:T(8,128)(2,1)S(1)}, bf16[2,256,128]{2,1,0:T(8,128)(2,1)S(1)}, f32[16,128]{1,0:T(8,128)S(1)}) custom-call(bf16[256,16,128]{2,1,0:T(8,128)(2,1)S(1)} %copy-done, bf16[256,16,128]{2,1,0:T(8,128)(2,1)S(1)} %copy-done.1, bf16[2,4,256,128]{3,2,1,0:T(8,128)(2,1)S(1)} %maximum_bitcast_fusion.pack_ref, ...), custom_call_target="tpu_custom_call" | custom-call | tf_op jit(solution)/shard_map/pallas_call | solution.py:351
  56.5 0.8 %copy.17 = bf16[256,2,128]{2,1,0:T(2,128)(2,1)} copy(bf16[256,2,128]{2,0,1:T(8,128)(2,1)S(1)} %bitcast.15) | data formatting | bytes 262144
  57.3 0.8 %copy.18 = bf16[256,2,128]{2,1,0:T(2,128)(2,1)} copy(bf16[256,2,128]{2,0,1:T(8,128)(2,1)S(1)} %bitcast.14) | data formatting | bytes 262144
  58.1 1.0 %copy.25 = bf16[256,16,128]{2,1,0:T(8,128)(2,1)} copy(bf16[256,16,128]{2,1,0:T(8,128)(2,1)S(1)} %get-tuple-element.24) | data formatting | bytes 2097152
  59.0 0.6 %copy.26 = f32[16,128]{1,0:T(8,128)} copy(f32[16,128]{1,0:T(8,128)S(1)} %get-tuple-element.27) | data formatting | bytes 16384
Async XLA Ops:
  0.6 2.3 %copy-start = (bf16[256,16,128]{2,1,0:T(8,128)(2,1)S(1)}, bf16[256,16,128]{2,1,0:T(8,128)(2,1)}, u32[]{:S(2)}) copy-start(bf16[256,16,128]{2,1,0:T(8,128)(2,1)} %q_rows.1) | copy-start | bytes 3145732
  0.6 2.3 %copy-start.1 = (bf16[256,16,128]{2,1,0:T(8,128)(2,1)S(1)}, bf16[256,16,128]{2,1,0:T(8,128)(2,1)}, u32[]{:S(2)}) copy-start(bf16[256,16,128]{2,1,0:T(8,128)(2,1)} %c_rows.1) | copy-start | bytes 3145732
  2.8 0.7 %copy-start.4 = (s32[256]{0:T(256)S(1)}, s32[256]{0:T(256)}, u32[]{:S(2)}) copy-start(s32[256]{0:T(256)} %param.12) | copy-start | bytes 3076
  3.5 0.7 %copy-start.2 = (f32[256,16]{0,1:T(8,128)S(1)}, f32[256,16]{0,1:T(8,128)}, u32[]{:S(2)}) copy-start(f32[256,16]{0,1:T(8,128)} %param.13) | copy-start | bytes 49156
  4.2 0.7 %copy-start.3 = (f32[16,128]{1,0:T(8,128)S(1)}, f32[16,128]{1,0:T(8,128)}, u32[]{:S(2)}) copy-start(f32[16,128]{1,0:T(8,128)} %gain_ref.1) | copy-start | bytes 24580
